TPU v7x, 128 devices: a whole 4x4x4 slice. The times are simulated.
128 devices in a mesh: lon: 16 (over y_hi, x, core), ch: 8 (over y_lo, z).
Axes of the slice: x: 4, y: 4 (y_hi: 2, y_lo: 2; y = y_hi * 2 + y_lo), z: 4, core: 2. Of those that a mesh axis runs over, the one named last changes fastest.
Arguments:
- latents: bfloat16 [96, 2, 1024, 640], P(None, None, 'lon', 'ch'), may hold values from -11 to 11
- next_latents: bfloat16 [96, 2, 1024, 640], P('ch', None, 'lon'), may hold values from -18 to 18
- timesteps: int32 [2], replicated, may hold values from 400 to 900
- resume_steps: int32 [2], replicated, may hold values from 40 to 100
- conv_weights: bfloat16 [2, 3, 3, 640, 640], replicated, may hold values from -0.078125 to 0.078125
- conv_bias: float32 [2, 640], replicated, may hold values from -1.5 to 1.5
- norm_gain: float32 [2, 640], replicated, may hold values from 0.1 to 1.9
- norm_shift: float32 [2, 640], replicated, may hold values from -1.5 to 1.5
- time_w1: float32 [320, 1280], replicated, may hold values from -0.3125 to 0.3125
- time_w2: float32 [1280, 640], replicated, may hold values from -0.15625 to 0.15625
Outputs:
- predicted_noise: bfloat16 [96, 2, 1024, 640], P('ch', None, 'lon')
- logprob: float32 [2], replicated
All inputs are finite; a program needn't handle non-finite values.
Results may differ from a plain program's by a relative error of at most 0.0044.
Values may be sent and summed in bfloat16 or wider, within the bound.
No kernel may reach another device: no remote copies, remote signals or barrier semaphores. Data moves between devices by JAX's collectives and lax.ppermute only.
A program may use at most 576 MiB of HBM per device.

v0:
```python
import math

import jax
import jax.numpy as jnp
from jax import lax
from jax.sharding import PartitionSpec as P

GROUPS = 32
LAT = 96


def with_halo(array, sides, width, wrap):
    for axis, dim in sides:
        size, length = (lax.axis_size(axis), array.shape[dim])
        up = [(i, (i + 1) % size) for i in range(size if wrap else size - 1)]
        down = [(j, i) for i, j in up]
        last = lax.slice_in_dim(array, length - width, length, axis=dim)
        first = lax.slice_in_dim(array, 0, width, axis=dim)
        before = lax.ppermute(last, axis, up)
        after = lax.ppermute(first, axis, down)
        array = jnp.concatenate([before, array, after], axis=dim)
    return array


def time_embed(timesteps, time_w1, time_w2):
    half = time_w1.shape[0] // 2
    freqs = jnp.exp(-math.log(10000.0) * jnp.arange(half, dtype=jnp.float32) / half)
    angles = timesteps.astype(jnp.float32)[:, None] * freqs[None, :]
    features = jnp.concatenate([jnp.cos(angles), jnp.sin(angles)], axis=1)
    hidden = jax.nn.silu(jnp.dot(features, time_w1, precision=lax.Precision.HIGHEST))
    return jnp.dot(hidden, time_w2, precision=lax.Precision.HIGHEST)


def group_sums(values, groups):
    rows, samples, cols, chans = values.shape
    grouped = values.reshape(rows, samples, cols, groups, chans // groups)
    return (jnp.sum(grouped, axis=(0, 2, 4)), jnp.sum(grouped * grouped, axis=(0, 2, 4)))


def normalize(values, sums, squares, total, gain, shift):
    groups = sums.shape[1]
    width = values.shape[3] // groups
    center = sums / total
    spread = squares / total - center * center
    factor = lax.rsqrt(spread + 1e-05)
    center = jnp.repeat(center, width, axis=1)[None, :, None, :]
    factor = jnp.repeat(factor, width, axis=1)[None, :, None, :]
    normed = (values - center) * factor * gain + shift
    return jax.nn.silu(normed).astype(jnp.bfloat16)


def convolve(padded, kernel):
    height = padded.shape[0] - 2
    across = padded.shape[2] - 2
    total = jnp.zeros((height, padded.shape[1], across, kernel.shape[3]), jnp.float32)
    for tap_row in range(3):
        for tap_col in range(3):
            piece = padded[tap_row : tap_row + height, :, tap_col : tap_col + across, :]
            total = total + lax.dot_general(
                piece,
                kernel[tap_row, tap_col],
                (((3,), (0,)), ((), ())),
                preferred_element_type=jnp.float32,
            )
    return total


def plan(steps):
    frac = steps.astype(jnp.float32) / 1000.0
    return jnp.cos((frac + 0.008) / 1.008 * (math.pi / 2.0)) ** 2


def step_terms(current, noise, following, timesteps, resume_steps):
    alpha = plan(timesteps)
    prior = plan(timesteps - resume_steps)
    variance = (1.0 - prior) / (1.0 - alpha) * (1.0 - alpha / prior)
    keep = (1.0 - prior) * jnp.sqrt(alpha / (prior * (1.0 - alpha)))
    shape_b = lambda v: v[None, :, None, None]
    clean = (current - shape_b(jnp.sqrt(1.0 - alpha)) * noise) / shape_b(jnp.sqrt(alpha))
    center = shape_b(jnp.sqrt(prior)) * clean + shape_b(keep) * noise
    diff = following - center
    return (jnp.sum(-(diff * diff) / (2.0 * shape_b(variance)), axis=(0, 2, 3)), variance)


def extend(field, width):
    beside_all = with_halo(field, (("lon", 2),), width, True)
    return with_halo(beside_all, (("ch", 0),), width, False)


def body(
    latents,
    next_latents,
    timesteps,
    resume_steps,
    conv_weights,
    conv_bias,
    norm_gain,
    norm_shift,
    time_w1,
    time_w2,
):
    lon_count = lax.axis_size("lon")
    cols = latents.shape[2]
    chans = conv_weights.shape[3]
    groups = GROUPS
    group_width = chans // groups
    total = latents.shape[0] * cols * lon_count * group_width
    temb = time_embed(timesteps, time_w1, time_w2)
    row_latents = lax.all_to_all(latents, "ch", split_axis=0, concat_axis=3, tiled=True)
    current = row_latents.astype(jnp.float32)
    sums, squares = lax.psum(group_sums(current, groups), ("lon", "ch"))
    first_input = normalize(current, sums, squares, total, norm_gain[0], norm_shift[0])
    hidden = (
        convolve(extend(first_input, 1), conv_weights[0]) + conv_bias[0] + temb[None, :, None, :]
    )
    sums, squares = lax.psum(group_sums(hidden, groups), ("lon", "ch"))
    second_input = extend(normalize(hidden, sums, squares, total, norm_gain[1], norm_shift[1]), 1)
    predicted_noise = (convolve(second_input, conv_weights[1]) + conv_bias[1] + current).astype(
        jnp.bfloat16
    )
    terms, variance = step_terms(
        current,
        predicted_noise.astype(jnp.float32),
        next_latents.astype(jnp.float32),
        timesteps,
        resume_steps,
    )
    terms = lax.psum(terms, ("lon", "ch"))
    logprob = (
        terms / (LAT * cols * lon_count * chans)
        - 0.5 * jnp.log(variance)
        - 0.5 * math.log(2.0 * math.pi)
    )
    return (predicted_noise, logprob)


def solution(mesh):
    return jax.shard_map(
        body,
        mesh=mesh,
        in_specs=(
            P(None, None, "lon", "ch"),
            P("ch", None, "lon", None),
            P(),
            P(),
            P(),
            P(),
            P(),
            P(),
            P(),
            P(),
        ),
        out_specs=(P("ch", None, "lon", None), P()),
        check_vma=False,
    )
```

profile of v0, /device:TPU:1, one launch (start us, length us, event | category | flops | bytes accessed | tf_op | source)
XLA Modules:
  0.0 419.2 jit_solution(10653846958296488773)
XLA Ops:
  0.6 6.7 %copy.22 = bf16[96,2,64,80]{3,2,1,0:T(8,128)(2,1)} copy(bf16[96,2,64,80]{0,3,2,1:T(8,128)(2,1)} %param.10) | data formatting | bytes 3932160 | tf_op args[0]
  7.4 7.0 %all-to-all-start = ((bf16[96,2,64,80]{3,2,1,0:T(8,128)(2,1)}), bf16[96,2,64,80]{3,2,1,0:T(8,128)(2,1)}, u32[]{:S(2)}, u32[]{:S(2)}) async-start(bf16[96,2,64,80]{3,2,1,0:T(8,128)(2,1)} %copy.22), calls=%async_computation | async-start | bytes 6291456 | tf_op jit(solution)/shard_map/all_to_all | solution.py:109
  14.8 0.1 multiply_cosine_fusion
  14.9 2.3 fusion.53
  17.2 1.7 fusion.48
  18.9 10.6 %slice_bitcast_fusion = (bf16[3,3,640,640]{3,2,1,0:T(8,128)(2,1)}, bf16[3,3,640,640]{3,2,1,0:T(8,128)(2,1)}) fusion(bf16[2,3,3,640,640]{4,3,2,1,0:T(8,128)(2,1)} %param.14), kind=kLoop, calls=%fused_computation | loop fusion | bytes 29491200 | tf_op jit(solution)/shard_map/squeeze | solution.py:118
  29.4 22.5 %all-to-all-done = bf16[96,2,64,80]{3,2,1,0:T(8,128)(2,1)} async-done(((bf16[96,2,64,80]{3,2,1,0:T(8,128)(2,1)}), bf16[96,2,64,80]{3,2,1,0:T(8,128)(2,1)}, u32[]{:S(2)}, u32[]{:S(2)}) %all-to-all-start) | async-done | bytes 1966112 | tf_op jit(solution)/shard_map/all_to_all | solution.py:109
  51.9 3.1 fusion
  55.1 5.4 %convert_bitcast_fusion = f32[12,2,64,8,80]{4,2,1,0,3:T(8,128)} fusion(bf16[8,12,2,64,80]{4,3,2,1,0:T(8,128)(2,1)} %bitcast.2), kind=kLoop, calls=%fused_computation.2 | loop fusion | flops 983040 | bytes 5898240 | tf_op jit(solution)/shard_map/convert_element_type | solution.py:110
  60.4 0.1 reduce_sum.55
  60.5 0.1 reduce_sum.61
  60.6 0.1 reduce_sum.59
  60.7 0.1 reduce_sum.62
  60.8 65.7 %all-reduce.1 = (f32[2,32]{1,0:T(2,128)S(1)}, f32[2,32]{1,0:T(2,128)S(1)}) all-reduce(f32[2,32]{1,0:T(2,128)S(1)} %reduce_sum.62, f32[2,32]{1,0:T(2,128)S(1)} %reduce_sum.59), channel_id=1, replica_groups=mesh['lon'=16,'ch'=8] {'lon','ch'}, use_global_device_ids=true, to_apply=%region_5.6 | all-reduce | flops 128 | bytes 1024 | tf_op jit(solution)/shard_map/psum | solution.py:111
  126.5 0.1 sub.60
  126.8 0.1 mul.151
  127.0 11.0 %copy.23 = f32[12,2,64,8,80]{4,3,2,1,0:T(8,128)} copy(f32[12,2,64,8,80]{4,2,1,0,3:T(8,128)} %convert_bitcast_fusion) | data formatting | bytes 7864320 | tf_op jit(solution)/shard_map/convert_element_type | solution.py:110
  137.9 7.1 %reshape.49 = f32[12,2,64,640]{3,2,1,0:T(8,128)} reshape(f32[12,2,64,8,80]{4,3,2,1,0:T(8,128)} %copy.23) | data formatting | bytes 7864320 | tf_op jit(solution)/shard_map/convert_element_type | solution.py:110
  145.0 3.4 multiply_convert_fusion.2
  148.4 0.1 fusion.67
  148.5 1.2 collective-permute-start
  149.6 0.4 collective-permute-start.1
  150.1 3.7 multiply_convert_fusion
  153.8 4.5 %copy.28 = bf16[12,2,64,8,80]{4,3,2,1,0:T(8,128)(2,1)} copy(bf16[12,2,64,8,80]{4,2,1,0,3:T(8,128)(2,1)S(1)} %multiply_convert_fusion) | data formatting | bytes 3932160 | tf_op jit(solution)/shard_map/convert_element_type | solution.py:49
  158.3 5.8 %convert_element_type.54 = bf16[12,2,64,640]{3,2,1,0:T(8,128)(2,1)} reshape(bf16[12,2,64,8,80]{4,3,2,1,0:T(8,128)(2,1)} %copy.28) | data formatting | bytes 3932160 | tf_op jit(solution)/shard_map/convert_element_type | solution.py:49
  164.1 5.6 %fusion.47 = f32[12,2,64,640]{3,2,1,0:T(8,128)} fusion(bf16[12,2,64,640]{3,2,1,0:T(8,128)(2,1)} %convert_element_type.54, bf16[3,3,640,640]{3,2,1,0:T(8,128)(2,1)} %get-tuple-element.23), kind=kOutput, calls=%fused_computation.77 | convolution fusion | flops 1258291200 | bytes 6717440 | tf_op jit(solution)/shard_map/dot_general | solution.py:59
  169.7 0.1 pad_maximum_fusion.15
  169.8 2.4 collective-permute-start.2
  172.2 1.6 collective-permute-start.3
  173.8 5.0 %fusion.34 = f32[12,2,64,640]{3,2,1,0:T(8,128)} fusion(bf16[12,2,64,640]{3,2,1,0:T(8,128)(2,1)S(1)} %multiply_convert_fusion.2, bf16[12,2,1,640]{3,2,1,0:T(2,128)(2,1)S(1)} %collective-permute-done, bf16[3,3,640,640]{3,2,1,0:T(8,128)(2,1)} %get-tuple-element.23), kind=kOutput, calls=%fused_computation.54 | convolution fusion | flops 1262223360 | bytes 6748160 | tf_op jit(solution)/shard_map/dot_general | solution.py:59
  178.8 3.8 fusion.32
  182.6 2.7 maximum_maximum_fusion
  185.3 3.9 fusion.36
  189.2 3.8 fusion.38
  192.9 3.8 fusion.40
  196.8 3.9 fusion.30
  200.6 3.8 fusion.28
  204.5 13.5 %fusion.64 = (f32[2,640]{1,0:T(2,128)S(1)}, f32[2,640]{1,0:T(2,128)S(1)}, f32[12,2,64,640]{3,2,1,0:T(8,128)}) fusion(f32[2,640]{1,0:T(2,128)S(1)} %fusion.48, f32[640]{0:T(1024)S(1)} %get-tuple-element.7, bf16[3,3,640,640]{3,2,1,0:T(8,128)(2,1)S(1)} %bitcast.153, bf16[13,2,66,640]{3,2,1,0:T(8,128)(2,1)S(1)} %get-tuple-element.29, ...), kind=kOutput, calls=%fused_computation.126 | convolution fusion | flops 1271068160 | bytes 38194176 | tf_op jit(solution)/shard_map/dot_general | solution.py:59
  218.0 0.1 reduce_sum.80
  218.1 0.1 reduce_sum.81
  218.2 0.1 reduce_sum.83
  218.3 0.1 reduce_sum.84
  218.4 70.4 %all-reduce = (f32[2,32]{1,0:T(2,128)S(1)}, f32[2,32]{1,0:T(2,128)S(1)}) all-reduce(f32[2,32]{1,0:T(2,128)S(1)} %reduce_sum.84, f32[2,32]{1,0:T(2,128)S(1)} %reduce_sum.81), channel_id=1, replica_groups=mesh['lon'=16,'ch'=8] {'lon','ch'}, use_global_device_ids=true, to_apply=%region_11.12 | all-reduce | flops 128 | bytes 1024 | tf_op jit(solution)/shard_map/psum | solution.py:116
  288.8 0.1 broadcast_in_dim.11
  288.9 0.1 mul.171
  289.0 0.1 sub.67
  289.2 3.5 multiply_convert_fusion.1
  292.7 0.1 fusion.66
  292.8 2.1 collective-permute-start.4
  294.9 5.1 %fusion.46 = f32[12,2,64,640]{3,2,1,0:T(8,128)} fusion(bf16[12,2,64,640]{3,2,1,0:T(8,128)(2,1)S(1)} %multiply_convert_fusion.1, bf16[3,3,640,640]{3,2,1,0:T(8,128)(2,1)} %get-tuple-element.22), kind=kOutput, calls=%fused_computation.67 | convolution fusion | flops 1258291200 | bytes 6717440 | tf_op jit(solution)/shard_map/dot_general | solution.py:59
  300.0 0.1 pad_maximum_fusion.12
  300.2 2.1 collective-permute-start.6
  302.3 1.3 collective-permute-start.7
  303.6 3.9 fusion.18
  307.5 3.8 fusion.16
  311.3 2.8 maximum_maximum_fusion.1
  314.1 3.7 fusion.20
  317.9 3.8 fusion.22
  321.7 3.9 fusion.24
  325.5 3.9 fusion.14
  329.4 3.9 fusion.12
  333.3 14.8 %fusion.9 = (f32[2]{0:T(128)S(1)}, bf16[12,2,64,640]{3,2,1,0:T(8,128)(2,1)}) fusion(f32[12,2,64,640]{3,2,1,0:T(8,128)S(1)} %copy-done.2, bf16[12,2,64,640]{3,2,1,0:T(8,128)(2,1)} %param.11, f32[2]{0:T(128)S(1)} %get-tuple-element.20, f32[2]{0:T(128)S(1)} %get-tuple-element.38, f32[2]{0:T(128)S(1)} %get-tuple-element.43, f32[2]{0:T(128)S(1)} %get-tuple-element.44, ...), kind=kOutput, calls=%fused_computation.21 | convolution fusion | flops 1281884160 | bytes 42113544 | tf_op jit(solution)/shard_map/dot_general | solution.py:59
  348.1 70.1 %psum.39 = f32[2]{0:T(128)S(1)} all-reduce(f32[2]{0:T(128)S(1)} %get-tuple-element.47), channel_id=1, replica_groups=mesh['lon'=16,'ch'=8] {'lon','ch'}, use_global_device_ids=true, to_apply=%region_13.14 | all-reduce | flops 2 | bytes 16 | tf_op jit(solution)/shard_map/psum | solution.py:128
  418.2 0.5 subtract_add_fusion
  (54 shorter events, 0.8 us)
Async XLA Ops:
  0.6 16.6 %copy-start = (f32[1280,640]{1,0:T(8,128)S(1)}, f32[1280,640]{1,0:T(8,128)}, u32[]{:S(2)}) copy-start(f32[1280,640]{1,0:T(8,128)} %param.19) | copy-start | bytes 9830404
  7.4 7.1 %copy-start.4 = (f32[2,640]{1,0:T(2,128)S(1)}, f32[2,640]{1,0:T(2,128)}, u32[]{:S(2)}) copy-start(f32[2,640]{1,0:T(2,128)} %param.17) | copy-start | bytes 15364
  7.4 7.1 %copy-start.5 = (f32[2,640]{1,0:T(2,128)S(1)}, f32[2,640]{1,0:T(2,128)}, u32[]{:S(2)}) copy-start(f32[2,640]{1,0:T(2,128)} %param.16) | copy-start | bytes 15364
  7.4 7.3 %copy-start.6 = (s32[2]{0:T(128)S(1)}, s32[2]{0:T(128)}, u32[]{:S(2)}) copy-start(s32[2]{0:T(128)} %param.12) | copy-start | bytes 28
  7.4 7.3 %copy-start.3 = (f32[2,640]{1,0:T(2,128)S(1)}, f32[2,640]{1,0:T(2,128)}, u32[]{:S(2)}) copy-start(f32[2,640]{1,0:T(2,128)} %param.15) | copy-start | bytes 15364
  7.4 7.3 %copy-start.7 = (s32[2]{0:T(128)S(1)}, s32[2]{0:T(128)}, u32[]{:S(2)}) copy-start(s32[2]{0:T(128)} %param.13) | copy-start | bytes 28
  7.4 44.5 %all-to-all-start = ((bf16[96,2,64,80]{3,2,1,0:T(8,128)(2,1)}), bf16[96,2,64,80]{3,2,1,0:T(8,128)(2,1)}, u32[]{:S(2)}, u32[]{:S(2)}) async-start(bf16[96,2,64,80]{3,2,1,0:T(8,128)(2,1)} %copy.22), calls=%async_computation | async-start | bytes 6291456 | tf_op jit(solution)/shard_map/all_to_all | solution.py:109
  148.5 21.2 %collective-permute-start = (bf16[12,2,1,640]{3,2,1,0:T(2,128)(2,1)S(1)}, bf16[12,2,1,640]{3,2,1,0:T(2,128)(2,1)S(1)}, u32[]{:S(2)}, u32[]{:S(2)}) collective-permute-start(bf16[12,2,1,640]{3,2,1,0:T(2,128)(2,1)S(1)} %get-tuple-element.34), channel_id=1, source_target_pairs={{0,8},{8,16},{16,24},{24,32},{32,40},{40,48},{48,56},{56,64},{64,7... | collective-permute-start | bytes 92168 | tf_op jit(solution)/shard_map/ppermute | solution.py:19
  149.6 20.0 %collective-permute-start.1 = (bf16[12,2,1,640]{3,2,1,0:T(2,128)(2,1)S(1)}, bf16[12,2,1,640]{3,2,1,0:T(2,128)(2,1)S(1)}, u32[]{:S(2)}, u32[]{:S(2)}) collective-permute-start(bf16[12,2,1,640]{3,2,1,0:T(2,128)(2,1)S(1)} %get-tuple-element.35), channel_id=1, source_target_pairs={{8,0},{16,8},{24,16},{32,24},{40,32},{48,40},{56,48},{64,56},{72,6... | collective-permute-start | bytes 92168 | tf_op jit(solution)/shard_map/ppermute | solution.py:20
  169.7 9.1 %slice-start = ((s8[7372800]{0:T(1024)(128)(4,1)}), s8[4194304]{0:T(1024)(128)(4,1)S(1)}, s32[]{:S(2)}) async-start(s8[7372800]{0:T(1024)(128)(4,1)} %bitcast.152), calls=%async_computation.1 | async-start | bytes 8388608
  169.8 12.7 %collective-permute-start.2 = (bf16[1,2,66,640]{3,2,1,0:T(8,128)(2,1)S(1)}, bf16[1,2,66,640]{3,2,1,0:T(8,128)(2,1)S(1)}, u32[]{:S(2)}, u32[]{:S(2)}) collective-permute-start(bf16[1,2,66,640]{3,2,1,0:T(8,128)(2,1)S(1)} %get-tuple-element.30), channel_id=1, source_target_pairs={{0,1},{1,2},{2,3},{3,4},{4,5},{5,6},{6,7},{8,9},{9,10},{10,11},{11... | collective-permute-start | bytes 506888 | tf_op jit(solution)/shard_map/ppermute | solution.py:19
  172.2 6.6 %slice-start.1 = ((s8[7372800]{0:T(1024)(128)(4,1)}), s8[3178496]{0:T(1024)(128)(4,1)S(1)}, s32[]{:S(2)}) async-start(s8[7372800]{0:T(1024)(128)(4,1)} %bitcast.152), calls=%async_computation.2 | async-start | bytes 6356992
  172.2 10.3 %collective-permute-start.3 = (bf16[1,2,66,640]{3,2,1,0:T(8,128)(2,1)S(1)}, bf16[1,2,66,640]{3,2,1,0:T(8,128)(2,1)S(1)}, u32[]{:S(2)}, u32[]{:S(2)}) collective-permute-start(bf16[1,2,66,640]{3,2,1,0:T(8,128)(2,1)S(1)} %get-tuple-element.31), channel_id=1, source_target_pairs={{1,0},{2,1},{3,2},{4,3},{5,4},{6,5},{7,6},{9,8},{10,9},{11,10},{12... | collective-permute-start | bytes 506888 | tf_op jit(solution)/shard_map/ppermute | solution.py:20
  289.2 14.4 %slice-start.2 = ((s8[7372800]{0:T(1024)(128)(4,1)}), s8[3178496]{0:T(1024)(128)(4,1)S(1)}, s32[]{:S(2)}) async-start(s8[7372800]{0:T(1024)(128)(4,1)} %bitcast.154), calls=%async_computation.3 | async-start | bytes 6356992
  292.8 7.2 %collective-permute-start.4 = (bf16[12,2,1,640]{3,2,1,0:T(2,128)(2,1)S(1)}, bf16[12,2,1,640]{3,2,1,0:T(2,128)(2,1)S(1)}, u32[]{:S(2)}, u32[]{:S(2)}) collective-permute-start(bf16[12,2,1,640]{3,2,1,0:T(2,128)(2,1)S(1)} %get-tuple-element.32), channel_id=1, source_target_pairs={{0,8},{8,16},{16,24},{24,32},{32,40},{40,48},{48,56},{56,64},{64,7... | collective-permute-start | bytes 92168 | tf_op jit(solution)/shard_map/ppermute | solution.py:19
  294.9 5.1 %collective-permute-start.5 = (bf16[12,2,1,640]{3,2,1,0:T(2,128)(2,1)S(1)}, bf16[12,2,1,640]{3,2,1,0:T(2,128)(2,1)S(1)}, u32[]{:S(2)}, u32[]{:S(2)}) collective-permute-start(bf16[12,2,1,640]{3,2,1,0:T(2,128)(2,1)S(1)} %get-tuple-element.33), channel_id=1, source_target_pairs={{8,0},{16,8},{24,16},{32,24},{40,32},{48,40},{56,48},{64,56},{72,6... | collective-permute-start | bytes 92168 | tf_op jit(solution)/shard_map/ppermute | solution.py:20
  294.9 8.7 %slice-start.3 = ((s8[7372800]{0:T(1024)(128)(4,1)}), s8[4194304]{0:T(1024)(128)(4,1)S(1)}, s32[]{:S(2)}) async-start(s8[7372800]{0:T(1024)(128)(4,1)} %bitcast.154), calls=%async_computation.4 | async-start | bytes 8388608
  300.2 11.2 %collective-permute-start.6 = (bf16[1,2,66,640]{3,2,1,0:T(8,128)(2,1)S(1)}, bf16[1,2,66,640]{3,2,1,0:T(8,128)(2,1)S(1)}, u32[]{:S(2)}, u32[]{:S(2)}) collective-permute-start(bf16[1,2,66,640]{3,2,1,0:T(8,128)(2,1)S(1)} %get-tuple-element.26), channel_id=1, source_target_pairs={{0,1},{1,2},{2,3},{3,4},{4,5},{5,6},{6,7},{8,9},{9,10},{10,11},{11... | collective-permute-start | bytes 506888 | tf_op jit(solution)/shard_map/ppermute | solution.py:19
  302.3 9.1 %collective-permute-start.7 = (bf16[1,2,66,640]{3,2,1,0:T(8,128)(2,1)S(1)}, bf16[1,2,66,640]{3,2,1,0:T(8,128)(2,1)S(1)}, u32[]{:S(2)}, u32[]{:S(2)}) collective-permute-start(bf16[1,2,66,640]{3,2,1,0:T(8,128)(2,1)S(1)} %get-tuple-element.27), channel_id=1, source_target_pairs={{1,0},{2,1},{3,2},{4,3},{5,4},{6,5},{7,6},{9,8},{10,9},{11,10},{12... | collective-permute-start | bytes 506888 | tf_op jit(solution)/shard_map/ppermute | solution.py:20
  329.4 3.9 copy-start.2
  333.3 85.4 %copy-start.1 = (f32[1280,640]{1,0:T(8,128)S(1)}, f32[1280,640]{1,0:T(8,128)}, u32[]{:S(2)}) copy-start(f32[1280,640]{1,0:T(8,128)} %param.19) | copy-start | bytes 9830404
where the time goes:
time: 425 us; the launch traced here: 419 us
  blocking collectives  206 us (48%)
  matrix products  97.8 us (23%)
  local copies, waits for them, and re-layouts  47.4 us (11%)
  other arithmetic  25.9 us (6%)
  waiting for transfers between devices  22.5 us (5%)
  starting transfers between devices  18 us (4%)
    dot_general x18, matrix products, convolve(): lax.dot_general(piece, kernel[tap_row, tap_col], (((3,), (0,)), ((), ()))...  93.8 us
    psum x1, blocking collectives, body(): sums, squares = lax.psum(group_sums(hidden, groups), ('lon', 'ch'))  70.4 us
    psum x1, blocking collectives, body(): terms = lax.psum(terms, ('lon', 'ch'))  70.1 us
    psum x1, blocking collectives, body(): sums, squares = lax.psum(group_sums(current, groups), ('lon', 'ch'))  65.7 us
    all_to_all x1, waiting for transfers between devices, body(): lax.all_to_all(latents, 'ch', split_axis=0, concat_axis=3, tiled=True)  22.5 us
    convert_element_type x2, local copies, waits for them, and re-layouts, body(): current = row_latents.astype(jnp.float32)  18 us
    convert_element_type x3, other arithmetic, normalize(): return jax.nn.silu(normed).astype(jnp.bfloat16)  10.6 us
    squeeze x1, local copies, waits for them, and re-layouts, body(): conv_weights[1]  10.6 us
  transfers between devices with their start and end apart: 9, of which 1 were waited for; matrix products, arithmetic and copies ran while one was open for 13% of the time, Pallas kernels for 0%

commit v1 on v0

v1 whole, which is shorter than its diff:
```python
import functools
import math

import jax
import jax.numpy as jnp
from jax import lax
from jax.experimental import pallas as pl
from jax.experimental.pallas import tpu as pltpu
from jax.sharding import PartitionSpec as P

GROUPS = 32
C = 640
LAT = 96
ROWS = 12
COLS = 64
SRC = 8
PART = C // SRC
WIDTH = C // GROUPS
TAPS = 9
F32 = jnp.float32
BF16 = jnp.bfloat16
VMEM = pl.BlockSpec(memory_space=pltpu.VMEM)
SMEM = pl.BlockSpec(memory_space=pltpu.SMEM)
ANY = pl.BlockSpec(memory_space=pl.ANY)
LIMIT = 56 * 2**20


def place(q, s):
    return 2 * q + 3 + 16 * s


def roll(x, by):
    by %= 128
    return x if by == 0 else pltpu.roll(x, by, 1)


def flip(x):
    n = x.shape[1]
    row = lax.broadcasted_iota(jnp.int32, (n, n), 0)
    col = lax.broadcasted_iota(jnp.int32, (n, n), 1)
    eye = jnp.where(row == col, 1.0, 0.0).astype(BF16)
    return lax.dot_general(eye, x, (((1,), (1,)), ((), ())), preferred_element_type=F32)


def lanes(rows):
    return lax.broadcasted_iota(jnp.int32, (rows, 128), 1)


def members(rows, first, base):
    chan = lax.broadcasted_iota(jnp.int32, (rows, 128), 0) + first
    low = (lanes(rows) - base) * WIDTH
    return (chan >= low) & (chan < low + WIDTH)


def silu(x):
    return 0.5 * x * (1.0 + jnp.tanh(0.5 * x))


def pack_kernel(
    part_ref, main_ref, above_ref, below_ref, left_ref, right_ref,
    pay0_ref, pay1_ref, sums_ref, halo, grid, total, square,
):
    d = pl.program_id(0)

    @pl.when(d == 0)
    def _():
        total[...] = jnp.zeros_like(total)
        square[...] = jnp.zeros_like(square)
        halo[...] = jnp.zeros_like(halo)
        grid[...] = jnp.zeros_like(grid)
        for s in range(2):
            halo[0, s, 8 : 8 + LAT, :] = left_ref[s].astype(F32)
            halo[1, s, 8 : 8 + LAT, :] = right_ref[s].astype(F32)

    start = 7 + d * ROWS
    for s in range(2):
        out = pay0_ref if s == 0 else pay1_ref
        for q in range(6):
            tile = flip(jnp.concatenate([main_ref[q, s], main_ref[q + 6, s]], axis=0))
            total[s] += tile
            square[s] += tile * tile
            out[0, q * PART : (q + 1) * PART, :] = tile.astype(BF16)
        edge = flip(jnp.concatenate([above_ref[0, s], below_ref[0, s]], axis=0))
        out[0, 6 * PART : 7 * PART, :] = edge.astype(BF16)
        at = place(-1, s)
        grid[pl.ds(at, 8, stride=2), :] = halo[0, s, pl.ds(start, 8), :]
        grid[pl.ds(at + 64, 8, stride=2), :] = halo[0, s, pl.ds(start + 6, 8), :]
        grid[pl.ds(at + 63, 8, stride=2), :] = halo[1, s, pl.ds(start, 8), :]
        grid[pl.ds(at - 1, 8, stride=2), :] = halo[1, s, pl.ds(start + 6, 8), :]
    pay0_ref[0, 7 * PART : 8 * PART, :] = flip(grid[...].astype(BF16)).astype(BF16)

    @pl.when(d == SRC - 1)
    def _():
        row = jnp.zeros((1, 128), F32)
        for s in range(2):
            for k, acc in ((0, total), (1, square)):
                column = jnp.sum(acc[s], axis=1, keepdims=True)
                own = members(PART, part_ref[0] * PART, 64 * k + 32 * s)
                row += jnp.sum(jnp.where(own, column, 0.0), axis=0, keepdims=True)
        sums_ref[...] = jnp.broadcast_to(row, sums_ref.shape)


def pack(part, latents, left, right):
    block = (ROWS, 2, COLS, PART)
    edge = (1, 2, COLS, PART)
    return pl.pallas_call(
        pack_kernel,
        grid=(SRC,),
        in_specs=[
            SMEM,
            pl.BlockSpec(block, lambda d: (d, 0, 0, 0)),
            pl.BlockSpec(edge, lambda d: (jnp.maximum(d * ROWS - 1, 0), 0, 0, 0)),
            pl.BlockSpec(edge, lambda d: (jnp.minimum(d * ROWS + ROWS, LAT - 1), 0, 0, 0)),
            pl.BlockSpec((2, LAT, PART), lambda d: (0, 0, 0)),
            pl.BlockSpec((2, LAT, PART), lambda d: (0, 0, 0)),
        ],
        out_specs=[
            pl.BlockSpec((1, 8 * PART, 128), lambda d: (d, 0, 0)),
            pl.BlockSpec((1, 7 * PART, 128), lambda d: (d, 0, 0)),
            pl.BlockSpec((128, 128), lambda d: (0, 0)),
        ],
        out_shape=[
            jax.ShapeDtypeStruct((SRC, 8 * PART, 128), BF16),
            jax.ShapeDtypeStruct((SRC, 7 * PART, 128), BF16),
            jax.ShapeDtypeStruct((128, 128), F32),
        ],
        scratch_shapes=[
            pltpu.VMEM((2, 2, LAT + 24, PART), F32),
            pltpu.VMEM((128, PART), F32),
            pltpu.VMEM((2, PART, 128), F32),
            pltpu.VMEM((2, PART, 128), F32),
        ],
        compiler_params=pltpu.CompilerParams(vmem_limit_bytes=LIMIT),
        name="pack_latents",
    )(part, latents, latents, latents, left, right)


def weight_kernel(w_ref, o_ref):
    for at in range(0, C, 128):
        o_ref[0, at : at + 128, :] = flip(w_ref[0, 0, :, at : at + 128]).astype(BF16)


def turn_weights(weights):
    taps = weights.reshape(2, TAPS, C, C)
    return pl.pallas_call(
        weight_kernel,
        grid=(2, TAPS),
        in_specs=[pl.BlockSpec((1, 1, C, C), lambda j, t: (j, t, 0, 0))],
        out_specs=pl.BlockSpec((1, C, C), lambda j, t: (j, 0, t)),
        out_shape=jax.ShapeDtypeStruct((2, C, TAPS * C), BF16),
        compiler_params=pltpu.CompilerParams(vmem_limit_bytes=LIMIT),
        name="turn_weights",
    )(taps)


def affine(sums_ref, par_ref, s, j, scale, offset):
    count = float(LAT * 1024 * WIDTH)
    row = jnp.sum(sums_ref[...], axis=0, keepdims=True)

    def of_channel(base):
        picked = jnp.where(members(C, 0, base), row, 0.0)
        return jnp.sum(picked, axis=1, keepdims=True) / count

    mean = of_channel(32 * s)
    spread = of_channel(64 + 32 * s) - mean * mean
    factor = lax.rsqrt(spread + 1e-05) * par_ref[:, 2 * j : 2 * j + 1]
    rest = par_ref[:, 2 * j + 1 : 2 * j + 2] - mean * factor
    scale[...] = jnp.broadcast_to(factor, scale.shape)
    offset[...] = jnp.broadcast_to(rest, offset.shape)


def spread_taps(xs, at, rows, tiles, edge, beside, s, part):
    lane = lanes(rows)
    low = lane < 64
    first = (lane == 0) | (lane == 64)
    last = (lane == 63) | (lane == 127)
    for q in range(-1, 7):
        if q == -1:
            tile = jnp.where(low, edge, roll(tiles[5], 64))
        elif q == 6:
            tile = jnp.where(low, roll(tiles[0], 64), edge)
        else:
            tile = tiles[q]
        side = roll(beside, -place(q, s))
        taps = (jnp.where(first, side, roll(tile, 1)), tile, jnp.where(last, side, roll(tile, -1)))
        for k, tap in enumerate(taps):
            if q == -1:
                tap = jnp.where(low & (part == 0), 0.0, tap)
            elif q == 6:
                tap = jnp.where((~low) & (part == SRC - 1), 0.0, tap)
            xs[pl.ds(k * C + at, rows), 128 * (q + 1) : 128 * (q + 2)] = tap.astype(BF16)


def product(wv, xs, n):
    x = jnp.concatenate([xs[:, n + 128 * i : n + 128 * i + 256] for i in range(3)], axis=0)
    return jnp.dot(wv[...], x, preferred_element_type=F32)


def first_kernel(
    s, part_ref, sums_ref, par_ref, recv_ref, beside_ref, w_hbm, *rest,
):
    if s == 1:
        before = rest[:5]
        rest = rest[5:]
    hid_ref, out_sums, to_right, to_left, to_next, to_prev, xs, wv, scale, offset, sem = rest
    weights = pltpu.make_async_copy(w_hbm.at[0], wv, sem)
    weights.start()
    part = part_ref[0]
    affine(sums_ref, par_ref, s, 0, scale, offset)

    @pl.loop(0, SRC)
    def _(b):
        at = pl.multiple_of(b * PART, PART)
        a, o = scale[pl.ds(at, PART), :], offset[pl.ds(at, PART), :]

        def act(x):
            return silu(x.astype(F32) * a + o)

        tiles = [act(recv_ref[b, q * PART : (q + 1) * PART, :]) for q in range(7)]
        spread_taps(xs, at, PART, tiles[:6], tiles[6], act(beside_ref[b]), s, part)

    weights.wait()
    bias = par_ref[:, 5 + s : 6 + s]
    for n in range(0, 768, 256):
        hid_ref[:, n : n + 256] = product(wv, xs, n) + bias

    row = jnp.zeros((1, 128), F32) if s == 0 else before[0][0:1, :]
    for at in range(0, C, 128):
        block = hid_ref[at : at + 128, :]
        pieces = [block[:, 128 * q : 128 * (q + 1)] for q in range(6)]
        for k in range(2):
            column = jnp.sum(sum(p * p if k else p for p in pieces), axis=1, keepdims=True)
            own = members(128, at, 64 * k + 32 * s)
            row += jnp.sum(jnp.where(own, column, 0.0), axis=0, keepdims=True)
        lane = lanes(128)
        right = jnp.zeros((128, 128), F32) if s == 0 else before[1][at : at + 128, :].astype(F32)
        left = jnp.zeros((128, 128), F32) if s == 0 else before[2][at : at + 128, :].astype(F32)
        for q in range(-1, 7):
            p = place(q, s)
            if q == -1:
                moved, whole = roll(pieces[5], 64), ((lane == p + 64), (lane == p - 1))
            elif q == 6:
                moved, whole = roll(pieces[0], 64), ((lane == p), (lane == p + 63))
            else:
                moved = pieces[q]
                whole = ((lane == p) | (lane == p + 64)), ((lane == p + 63) | (lane == p - 1))
            right = jnp.where(whole[0], roll(moved, p - 63), right)
            left = jnp.where(whole[1], roll(moved, p + 63), left)
        to_right[at : at + 128, :] = right.astype(BF16)
        to_left[at : at + 128, :] = left.astype(BF16)
        if s == 0:
            after, ahead = roll(pieces[5], 64), pieces[0]
        else:
            low = lane < 64
            after = jnp.where(low, before[3][at : at + 128, :].astype(F32), pieces[5])
            ahead = jnp.where(low, before[4][at : at + 128, :].astype(F32), roll(pieces[0], 64))
        to_next[at : at + 128, :] = after.astype(BF16)
        to_prev[at : at + 128, :] = ahead.astype(BF16)
    out_sums[...] = jnp.broadcast_to(row, out_sums.shape)


def first_conv(s, part, sums, params, recv, beside, weights, before):
    tile = jax.ShapeDtypeStruct((C, 128), BF16)
    return pl.pallas_call(
        functools.partial(first_kernel, s),
        in_specs=[SMEM, VMEM, VMEM, VMEM, VMEM, ANY] + [VMEM] * len(before),
        out_specs=[VMEM] * 6,
        out_shape=[
            jax.ShapeDtypeStruct((C, 768), F32),
            jax.ShapeDtypeStruct((128, 128), F32),
            tile, tile, tile, tile,
        ],
        scratch_shapes=[
            pltpu.VMEM((3 * C, 1024), BF16),
            pltpu.VMEM((C, TAPS * C), BF16),
            pltpu.VMEM((C, 128), F32),
            pltpu.VMEM((C, 128), F32),
            pltpu.SemaphoreType.DMA,
        ],
        compiler_params=pltpu.CompilerParams(vmem_limit_bytes=LIMIT),
        cost_estimate=pl.CostEstimate(
            flops=2 * 768 * C * C * 9, bytes_accessed=12_000_000, transcendentals=0
        ),
        name=f"first_conv_{s}",
    )(part, sums, params, recv, beside, weights, *before)


def second_kernel(
    part_ref, coef_ref, sums_ref, par_ref, near_ref, up_ref, down_ref, prev_ref, next_ref,
    hid0, hid1, w_hbm, recv0, recv1, target_hbm,
    noise_ref, out_ref,
    xs, wv, lat0, lat1, target, scale, offset, sems,
):
    copies = [
        pltpu.make_async_copy(w_hbm.at[1], wv, sems.at[0]),
        pltpu.make_async_copy(recv0.at[:, 0 : 6 * PART, :], lat0, sems.at[1]),
        pltpu.make_async_copy(recv1.at[:, 0 : 6 * PART, :], lat1, sems.at[2]),
        pltpu.make_async_copy(target_hbm, target, sems.at[3]),
    ]
    for copy in copies:
        copy.start()
    part = part_ref[0]
    result = jnp.zeros((1, 128), F32)
    for s in range(2):
        hid = (hid0, hid1)[s]
        lat = (lat0, lat1)[s]
        affine(sums_ref, par_ref, s, 1, scale, offset)

        @pl.loop(0, SRC)
        def _(b):
            at = pl.multiple_of(b * PART, PART)
            rows = pl.ds(at, PART)
            a, o = scale[rows, :], offset[rows, :]
            lane = lanes(PART)
            low = lane < 64

            def act(x):
                return silu(x.astype(F32) * a + o)

            tiles = [act(hid[rows, 128 * q : 128 * (q + 1)]) for q in range(6)]
            above, below = prev_ref[rows, :].astype(F32), next_ref[rows, :].astype(F32)
            if s == 0:
                edge = jnp.where(low, above, roll(below, 64))
            else:
                edge = jnp.where(low, roll(above, 64), below)
            beside = near_ref[rows, :].astype(F32)
            p = place(-1, s)
            corner = roll(up_ref[rows, :].astype(F32), 52)
            beside = jnp.where((lane == p) | (lane == p + 63), corner, beside)
            p = place(6, s)
            corner = roll(down_ref[rows, :].astype(F32), 76)
            beside = jnp.where((lane == p + 64) | (lane == p - 1), corner, beside)
            spread_taps(xs, at, PART, tiles, act(edge), act(beside), s, part)

        if s == 0:
            copies[0].wait()
        bias = par_ref[:, 4:5]
        if s == 0:
            for copy in copies[1:]:
                copy.wait()
        acc = jnp.zeros((128, 128), F32)
        keep, gain = coef_ref[2 * s], coef_ref[2 * s + 1]
        for n in range(0, 768, 256):
            out = product(wv, xs, n) + bias
            for half in range(2):
                q = n // 128 + half
                mine = lat[:, q * PART : (q + 1) * PART, :].reshape(C, 128).astype(F32)
                noise = (out[:, 128 * half : 128 * (half + 1)] + mine).astype(BF16)
                center = keep * mine + gain * noise.astype(F32)
                want = jnp.concatenate([target[q, s], target[q + 6, s]], axis=0)
                for at in range(0, C, 128):
                    turned = flip(noise[at : at + 128, :]).astype(BF16)
                    noise_ref[q, s, :, at : at + 128] = turned[0:64]
                    noise_ref[q + 6, s, :, at : at + 128] = turned[64:128]
                    diff = flip(want[:, at : at + 128]) - center[at : at + 128, :]
                    acc += diff * diff
        value = jnp.sum(acc, axis=(0, 1), keepdims=True)
        result = jnp.where(lanes(1) == s, value, result)
    out_ref[...] = jnp.broadcast_to(result, out_ref.shape)


def second_conv(part, coef, sums, params, tiles, hidden, weights, recv, target):
    return pl.pallas_call(
        second_kernel,
        in_specs=[SMEM, SMEM] + [VMEM] * 9 + [ANY] * 4,
        out_specs=[VMEM] * 2,
        out_shape=[
            jax.ShapeDtypeStruct((ROWS, 2, COLS, C), BF16),
            jax.ShapeDtypeStruct((128, 128), F32),
        ],
        scratch_shapes=[
            pltpu.VMEM((3 * C, 1024), BF16),
            pltpu.VMEM((C, TAPS * C), BF16),
            pltpu.VMEM((SRC, 6 * PART, 128), BF16),
            pltpu.VMEM((SRC, 6 * PART, 128), BF16),
            pltpu.VMEM((ROWS, 2, COLS, C), BF16),
            pltpu.VMEM((C, 128), F32),
            pltpu.VMEM((C, 128), F32),
            pltpu.SemaphoreType.DMA((4,)),
        ],
        compiler_params=pltpu.CompilerParams(vmem_limit_bytes=LIMIT),
        cost_estimate=pl.CostEstimate(
            flops=4 * 768 * C * C * 9, bytes_accessed=20_000_000, transcendentals=0
        ),
        name="second_conv",
    )(part, coef, sums, params, *tiles, *hidden, weights, *recv, target)


def time_embed(timesteps, time_w1, time_w2):
    half = time_w1.shape[0] // 2
    freqs = jnp.exp(-math.log(10000.0) * jnp.arange(half, dtype=F32) / half)
    angles = timesteps.astype(F32)[:, None] * freqs[None, :]
    features = jnp.concatenate([jnp.cos(angles), jnp.sin(angles)], axis=1)
    hidden = jax.nn.silu(jnp.dot(features, time_w1, precision=lax.Precision.HIGHEST))
    return jnp.dot(hidden, time_w2, precision=lax.Precision.HIGHEST)


def plan(steps):
    frac = steps.astype(F32) / 1000.0
    return jnp.cos((frac + 0.008) / 1.008 * (math.pi / 2.0)) ** 2


def everywhere(rows):
    got = lax.all_to_all(rows.reshape(128, 1, 128), ("lon", "ch"), 0, 0, tiled=True)
    return got.reshape(128, 128)


def ring(axis, step, wrap):
    size = lax.axis_size(axis)
    return [(i, (i + step) % size) for i in range(size) if wrap or 0 <= i + step < size]


def swap(array, axis):
    return lax.all_to_all(array, axis, split_axis=0, concat_axis=0, tiled=True)


def body(
    latents, next_latents, timesteps, resume_steps, conv_weights, conv_bias,
    norm_gain, norm_shift, time_w1, time_w2,
):
    part = lax.axis_index("ch").astype(jnp.int32).reshape(1)
    last = latents[:, :, COLS - 1, :].transpose(1, 0, 2)
    first = latents[:, :, 0, :].transpose(1, 0, 2)
    left = lax.ppermute(last, "lon", ring("lon", 1, True))
    right = lax.ppermute(first, "lon", ring("lon", -1, True))
    pay0, pay1, sums = pack(part, latents, left, right)
    pay0, pay1, sums, conv_weights, time_w1 = lax.optimization_barrier(
        (pay0, pay1, sums, conv_weights, time_w1)
    )
    recv0 = swap(pay0, "ch")
    recv1 = swap(pay1, "ch")
    sums = everywhere(sums)
    turned = turn_weights(conv_weights)

    temb = time_embed(timesteps, time_w1, time_w2)
    columns = [
        norm_gain[0], norm_shift[0], norm_gain[1], norm_shift[1], conv_bias[1],
        conv_bias[0] + temb[0], conv_bias[0] + temb[1],
    ]
    params = jnp.pad(jnp.stack(columns, axis=1), ((0, 0), (0, 128 - len(columns))))

    alpha = plan(timesteps)
    prior = plan(timesteps - resume_steps)
    variance = (1.0 - prior) / (1.0 - alpha) * (1.0 - alpha / prior)
    keep = (1.0 - prior) * jnp.sqrt(alpha / (prior * (1.0 - alpha)))
    ratio = jnp.sqrt(prior) / jnp.sqrt(alpha)
    coef = jnp.stack([ratio, keep - ratio * jnp.sqrt(1.0 - alpha)], axis=1).reshape(4)

    beside = recv0[:, 7 * PART : 8 * PART, :]
    hid0, *before = first_conv(0, part, sums, params, recv0, beside, turned, ())
    hid1, sums, to_right, to_left, to_next, to_prev = first_conv(
        1, part, sums, params, recv1, beside, turned, before
    )
    from_left = lax.ppermute(to_right, "lon", ring("lon", 1, True))
    from_right = lax.ppermute(to_left, "lon", ring("lon", -1, True))
    from_prev = lax.ppermute(to_next, "ch", ring("ch", 1, False))
    from_next = lax.ppermute(to_prev, "ch", ring("ch", -1, False))
    near = from_left + from_right
    up = lax.ppermute(near, "ch", ring("ch", 1, False))
    down = lax.ppermute(near, "ch", ring("ch", -1, False))
    sums = everywhere(sums)
    noise, terms = second_conv(
        part, coef, sums, params, (near, up, down, from_prev, from_next),
        (hid0, hid1), turned, (recv0, recv1), next_latents,
    )
    squares = jnp.sum(everywhere(terms), axis=0)[:2]
    logprob = (
        -squares / (2.0 * variance) / float(LAT * 1024 * C)
        - 0.5 * jnp.log(variance)
        - 0.5 * math.log(2.0 * math.pi)
    )
    return (noise, logprob)


def solution(mesh):
    return jax.shard_map(
        body,
        mesh=mesh,
        in_specs=(
            P(None, None, "lon", "ch"),
            P("ch", None, "lon", None),
            P(), P(), P(), P(), P(), P(), P(), P(),
        ),
        out_specs=(P("ch", None, "lon", None), P()),
        check_vma=False,
    )
```

time: 425 us -> 210 us (0.49); the launches traced: 419 us -> 209 us
  blocking collectives: 206 us -> 36 us
  matrix products: 97.8 us -> 3.94 us
  Pallas kernels: 0 us -> 92.8 us
  local copies, waits for them, and re-layouts: 47.4 us -> 13 us
  other arithmetic: 25.9 us -> 1.05 us
  starting transfers between devices: 18 us -> 36.9 us
    psum x3 -> x0, blocking collectives: 206 us -> none  [the longest x1 70.4 us: body(): sums, squares = lax.psum(group_sums(hidden, groups), ('lon', 'ch'))]
    dot_general x18 -> x0, matrix products: 93.8 us -> none  [convolve(): lax.dot_general(piece, kernel[tap_row, tap_col], (((3,), (0,)), ((), ()))...]
    pallas_call x0 -> x5, Pallas kernels: none -> 92.8 us  [the longest x1 39.4 us: second_conv(): pl.pallas_call(second_kernel, in_specs=[SMEM, SMEM] + [VMEM] * 9 + [ANY]...]
    all_to_all x0 -> x2, blocking collectives: none -> 36 us  [everywhere(): lax.all_to_all(rows.reshape(128, 1, 128), ('lon', 'ch'), 0, 0, tiled=True)]
    convert_element_type x4 -> x0, local copies, waits for them, and re-layouts: 28.4 us -> none  [the longest x2 18 us: body(): current = row_latents.astype(jnp.float32)]
    convert_element_type x5 -> x1, other arithmetic: 16 us -> 0.01 us  [plan(): frac = steps.astype(F32) / 1000.0]
    all_to_all x1 -> x3, starting transfers between devices: 7.02 us -> 21.2 us  [the longest x1 12.5 us: everywhere(): lax.all_to_all(rows.reshape(128, 1, 128), ('lon', 'ch'), 0, 0, tiled=True)]
    squeeze x1 -> x0, local copies, waits for them, and re-layouts: 10.6 us -> none  [body(): conv_weights[1]]
  transfers between devices with their start and end apart: 9 -> 11, of which waited for: 1 -> 2; matrix products, arithmetic and copies ran while one was open for 13% -> 7% of each run, Pallas kernels for 0% -> 15%
where the time goes in v1:
time: 210 us; the launch traced here: 209 us
  Pallas kernels  92.8 us (44%)
  starting transfers between devices  36.9 us (18%)
  blocking collectives  36 us (17%)
  waiting for transfers between devices  24.1 us (11%)
  local copies, waits for them, and re-layouts  13 us (6%)
  matrix products  3.94 us (2%)
    pallas_call x1, Pallas kernels, second_conv(): pl.pallas_call(second_kernel, in_specs=[SMEM, SMEM] + [VMEM] * 9 + [ANY]...  39.4 us
    all_to_all x2, blocking collectives, everywhere(): lax.all_to_all(rows.reshape(128, 1, 128), ('lon', 'ch'), 0, 0, tiled=True)  36 us
    pallas_call x2, Pallas kernels, first_conv(): pl.pallas_call(functools.partial(first_kernel, s), in_specs=[SMEM, VMEM,...  26.4 us
    pallas_call x1, Pallas kernels, turn_weights(): pl.pallas_call(weight_kernel, grid=(2, TAPS), in_specs=[pl.BlockSpec((1,...  19.1 us
    all_to_all x2, waiting for transfers between devices, swap(): return lax.all_to_all(array, axis, split_axis=0, concat_axis=0, tiled=True)  15.2 us
    all_to_all x1, starting transfers between devices, everywhere(): lax.all_to_all(rows.reshape(128, 1, 128), ('lon', 'ch'), 0, 0, tiled=True)  12.5 us
    all_to_all x1, waiting for transfers between devices, everywhere(): lax.all_to_all(rows.reshape(128, 1, 128), ('lon', 'ch'), 0, 0, tiled=True)  8.87 us
    all_to_all x2, starting transfers between devices, swap(): return lax.all_to_all(array, axis, split_axis=0, concat_axis=0, tiled=True)  8.71 us
  transfers between devices with their start and end apart: 11, of which 2 were waited for; matrix products, arithmetic and copies ran while one was open for 7% of the time, Pallas kernels for 15%

profile of v1, /device:TPU:1, one launch (start us, length us, event | category | flops | bytes accessed | tf_op | source)
XLA Modules:
  0.0 208.7 jit_solution(17783783139870292009)
XLA Ops:
  0.6 0.0 copy-start
  0.6 1.0 fusion.14
  1.6 0.1 copy.41
  1.7 2.7 %collective-permute-start = (bf16[2,96,80]{2,1,0:T(8,128)(2,1)S(1)}, bf16[2,96,80]{2,1,0:T(8,128)(2,1)S(1)}, u32[]{:S(2)}, u32[]{:S(2)}) collective-permute-start(bf16[2,96,80]{2,1,0:T(8,128)(2,1)S(1)} %bitcast.46), channel_id=1, source_target_pairs={{0,8},{8,16},{16,24},{24,32},{32,40},{40,48},{48,56},{56,64},{64,7... | collective-permute-start | bytes 92168 | tf_op jit(solution)/shard_map/ppermute | solution.py:424
  4.4 0.1 copy.42
  4.5 0.1 collective-permute-start.1
  4.6 6.6 %copy.34.main_ref.above_ref.below_ref = bf16[96,2,64,80]{3,2,1,0:T(8,128)(2,1)} copy(bf16[96,2,64,80]{0,3,2,1:T(8,128)(2,1)} %param.10) | data formatting | bytes 3932160 | tf_op args[0]
  11.1 0.0 collective-permute-done.left_ref
  11.2 0.0 collective-permute-done.1.right_ref
  11.2 0.0 copy-start.5
  11.2 0.6 copy-done.4
  11.8 0.0 copy-done.5
  11.8 7.9 %pack_latents.1 = (bf16[8,640,128]{2,1,0:T(8,128)(2,1)}, bf16[8,560,128]{2,1,0:T(8,128)(2,1)}, f32[128,128]{1,0:T(8,128)}) custom-call(s32[1]{0:T(128)} %bitcast.part_ref, bf16[96,2,64,80]{3,2,1,0:T(8,128)(2,1)} %copy.34.main_ref.above_ref.below_ref, bf16[96,2,64,80]{3,2,1,0:T(8,128)(2,1)} %copy.34.main_ref.above_ref.below_ref, ...), custom_call_target="tpu_custom_call" | custom-call | tf_op jit(solution)/shard_map/pack_latents/pallas_call | solution.py:106
  19.7 0.0 copy-start.9
  19.7 0.0 copy-start.8
  19.8 21.8 %all_to_all.25 = f32[128,1,128]{2,1,0:T(1,128)} all-to-all(f32[128,1,128]{2,1,0:T(1,128)} %bitcast.45), channel_id=1, replica_groups=mesh['lon'=16,'ch'=8] {'lon','ch'}, dimensions={0} | all-to-all | bytes 131072 | tf_op jit(solution)/shard_map/all_to_all | solution.py:404
  41.5 4.3 %all-to-all-start.2 = ((bf16[8,640,128]{2,1,0:T(8,128)(2,1)}), bf16[8,640,128]{2,1,0:T(8,128)(2,1)}, u32[]{:S(2)}, u32[]{:S(2)}) async-start(bf16[8,640,128]{2,1,0:T(8,128)(2,1)} %get-tuple-element.30), calls=%async_computation.2 | async-start | bytes 2621440 | tf_op jit(solution)/shard_map/all_to_all | solution.py:414
  45.8 0.0 copy-done.9
  45.8 0.1 multiply_cosine_fusion
  46.0 0.0 copy-done.8
  46.0 2.3 %fusion.5 = f32[2,1280]{1,0:T(2,128)S(1)} fusion(f32[320,1280]{1,0:T(8,128)} %param.18, f32[2,160]{1,0:T(2,128)S(1)} %get-tuple-element.58, f32[2,160]{1,0:T(2,128)S(1)} %get-tuple-element.57), kind=kOutput, calls=%fused_computation.6 | convolution fusion | flops 9831040 | bytes 1651200 | tf_op jit(solution)/shard_map/dot_general | solution.py:394
  48.3 15.2 %all-to-all-done.2.recv_ref.recv0 = bf16[8,640,128]{2,1,0:T(8,128)(2,1)} async-done(((bf16[8,640,128]{2,1,0:T(8,128)(2,1)}), bf16[8,640,128]{2,1,0:T(8,128)(2,1)}, u32[]{:S(2)}, u32[]{:S(2)}) %all-to-all-start.2) | async-done | bytes 1310752 | tf_op jit(solution)/shard_map/all_to_all | solution.py:414
  63.5 4.4 %all-to-all-start.1 = ((bf16[8,560,128]{2,1,0:T(8,128)(2,1)}), bf16[8,560,128]{2,1,0:T(8,128)(2,1)}, u32[]{:S(2)}, u32[]{:S(2)}) async-start(bf16[8,560,128]{2,1,0:T(8,128)(2,1)} %get-tuple-element.29), calls=%async_computation.1 | async-start | bytes 2293760 | tf_op jit(solution)/shard_map/all_to_all | solution.py:414
  68.0 0.0 copy-done
  68.0 0.0 copy-start.6
  68.0 0.0 copy-start.7
  68.0 1.7 fusion
  69.7 0.0 copy-done.6
  69.7 0.0 copy-done.7
  69.7 0.9 copy.38
  70.6 19.1 %turn_weights.1.w_hbm = bf16[2,640,5760]{2,1,0:T(8,128)(2,1)} custom-call(bf16[2,9,640,640]{3,2,1,0:T(8,128)(2,1)} %bitcast.39), custom_call_target="tpu_custom_call" | custom-call | tf_op jit(solution)/shard_map/turn_weights/pallas_call | solution.py:145
  89.7 0.0 copy-done.1
  89.7 0.8 pad.4.par_ref
  90.5 1.6 slice.51.beside_ref
  92.1 13.0 %first_conv_0.1 = (f32[640,768]{1,0:T(8,128)}, f32[128,128]{1,0:T(8,128)}, bf16[640,128]{1,0:T(8,128)(2,1)}, bf16[640,128]{1,0:T(8,128)(2,1)}, bf16[640,128]{1,0:T(8,128)(2,1)}, /*index=5*/bf16[640,128]{1,0:T(8,128)(2,1)}) custom-call(s32[1]{0:T(128)} %bitcast.part_ref, f32[128,128]{1,0:T(8,128)} %bitcast.40, f32[640,128]{1,0:T(8,128)} %pad.4.par_ref, ...), custom_call_target="tpu_custom_call" | custom-call | flops 5662310400 | bytes 12000000 | tf_op jit(solution)/shard_map/first_conv_0/pallas_call | solution.py:264
  105.1 0.0 all-to-all-done.1.recv_ref.recv1
  105.1 0.0 copy-start.10
  105.1 13.4 %first_conv_1.1 = (f32[640,768]{1,0:T(8,128)}, f32[128,128]{1,0:T(8,128)}, bf16[640,128]{1,0:T(8,128)(2,1)}, bf16[640,128]{1,0:T(8,128)(2,1)}, bf16[640,128]{1,0:T(8,128)(2,1)}, /*index=5*/bf16[640,128]{1,0:T(8,128)(2,1)}) custom-call(s32[1]{0:T(128)} %bitcast.part_ref, f32[128,128]{1,0:T(8,128)} %bitcast.41, f32[640,128]{1,0:T(8,128)} %pad.4.par_ref, ...), custom_call_target="tpu_custom_call" | custom-call | flops 5662310400 | bytes 12000000 | tf_op jit(solution)/shard_map/first_conv_1/pallas_call | solution.py:264
  118.5 0.8 collective-permute-start.2
  119.3 0.2 collective-permute-start.3
  119.5 0.0 copy-done.10
  119.5 0.1 fusion.11
  119.6 4.0 %collective-permute-start.6 = (bf16[640,128]{1,0:T(8,128)(2,1)}, bf16[640,128]{1,0:T(8,128)(2,1)}, u32[]{:S(2)}, u32[]{:S(2)}) collective-permute-start(bf16[640,128]{1,0:T(8,128)(2,1)} %get-tuple-element.40), channel_id=1, source_target_pairs={{0,1},{1,2},{2,3},{3,4},{4,5},{5,6},{6,7},{8,9},{9,10},{10,11},{11... | collective-permute-start | bytes 491528 | tf_op jit(solution)/shard_map/ppermute | solution.py:456
  123.6 1.3 collective-permute-start.7
  124.9 0.0 collective-permute-done.2
  124.9 0.0 collective-permute-done.3
  124.9 0.0 copy-start.2
  125.0 1.3 collective-permute-start.5
  126.3 5.3 %collective-permute-start.4 = (bf16[640,128]{1,0:T(8,128)(2,1)S(1)}, bf16[640,128]{1,0:T(8,128)(2,1)}, u32[]{:S(2)}, u32[]{:S(2)}) collective-permute-start(bf16[640,128]{1,0:T(8,128)(2,1)S(1)} %add.49.near_ref), channel_id=1, source_target_pairs={{0,1},{1,2},{2,3},{3,4},{4,5},{5,6},{6,7},{8,9},{9,10},{10,11},{11... | collective-permute-start | bytes 491528 | tf_op jit(solution)/shard_map/ppermute | solution.py:459
  131.5 0.1 subtract_bitcast_fusion
  131.6 12.5 %all-to-all-start.3 = ((f32[128,1,128]{2,1,0:T(1,128)}), f32[128,1,128]{2,1,0:T(1,128)S(1)}, u32[]{:S(2)}, u32[]{:S(2)}) async-start(f32[128,1,128]{2,1,0:T(1,128)} %bitcast.42), calls=%async_computation.3 | async-start | bytes 131072 | tf_op jit(solution)/shard_map/all_to_all | solution.py:404
  144.1 0.1 copy.31
  144.2 0.6 reshape.72.coef_ref
  144.9 8.9 %all-to-all-done.3 = f32[128,1,128]{2,1,0:T(1,128)S(1)} async-done(((f32[128,1,128]{2,1,0:T(1,128)}), f32[128,1,128]{2,1,0:T(1,128)S(1)}, u32[]{:S(2)}, u32[]{:S(2)}) %all-to-all-start.3) | async-done | bytes 65568 | tf_op jit(solution)/shard_map/all_to_all | solution.py:404
  153.7 0.0 collective-permute-done.6.prev_ref
  153.7 0.0 collective-permute-done.7.next_ref
  153.7 0.0 collective-permute-done.5.down_ref
  153.8 0.0 collective-permute-done.4.up_ref
  153.8 0.0 copy-done.2
  153.8 0.6 copy-done.3
  154.4 39.4 %second_conv.1 = (bf16[12,2,64,640]{3,2,1,0:T(8,128)(2,1)}, f32[128,128]{1,0:T(8,128)}) custom-call(s32[1]{0:T(128)} %bitcast.part_ref, f32[4]{0:T(128)} %reshape.72.coef_ref, f32[128,128]{1,0:T(8,128)} %bitcast.43, f32[640,128]{1,0:T(8,128)} %pad.4.par_ref, bf16[640,128]{1,0:T(8,128)(2,1)} %copy-done.2, bf16[640,128]{1,0:T(8,128)(2,1)} %collective-permute-done.4.up_ref, ...), custom_call_target="tpu_custom_call" | custom-call | flops 11324620800 | bytes 20000000 | tf_op jit(solution)/shard_map/second_conv/pallas_call | solution.py:363
  193.7 14.3 %all_to_all.26 = f32[128,1,128]{2,1,0:T(1,128)S(1)} all-to-all(f32[128,1,128]{2,1,0:T(1,128)} %bitcast.44), channel_id=1, replica_groups=mesh['lon'=16,'ch'=8] {'lon','ch'}, dimensions={0} | all-to-all | bytes 131072 | tf_op jit(solution)/shard_map/all_to_all | solution.py:404
  208.0 0.2 reduce_sum.9
  208.2 0.6 subtract_add_fusion
  (10 shorter events, 0.1 us)
Async XLA Ops:
  0.6 67.3 %copy-start = (f32[1280,640]{1,0:T(8,128)S(1)}, f32[1280,640]{1,0:T(8,128)}, u32[]{:S(2)}) copy-start(f32[1280,640]{1,0:T(8,128)} %param.19) | copy-start | bytes 9830404
  1.7 9.4 %collective-permute-start = (bf16[2,96,80]{2,1,0:T(8,128)(2,1)S(1)}, bf16[2,96,80]{2,1,0:T(8,128)(2,1)S(1)}, u32[]{:S(2)}, u32[]{:S(2)}) collective-permute-start(bf16[2,96,80]{2,1,0:T(8,128)(2,1)S(1)} %bitcast.46), channel_id=1, source_target_pairs={{0,8},{8,16},{16,24},{24,32},{32,40},{40,48},{48,56},{56,64},{64,7... | collective-permute-start | bytes 92168 | tf_op jit(solution)/shard_map/ppermute | solution.py:424
  4.5 6.7 %collective-permute-start.1 = (bf16[2,96,80]{2,1,0:T(8,128)(2,1)S(1)}, bf16[2,96,80]{2,1,0:T(8,128)(2,1)S(1)}, u32[]{:S(2)}, u32[]{:S(2)}) collective-permute-start(bf16[2,96,80]{2,1,0:T(8,128)(2,1)S(1)} %bitcast.47), channel_id=1, source_target_pairs={{0,120},{8,0},{16,8},{24,16},{32,24},{40,32},{48,40},{56,48},{64,5... | collective-permute-start | bytes 92168 | tf_op jit(solution)/shard_map/ppermute | solution.py:425
  11.1 0.6 copy-start.4
  11.2 0.6 copy-start.5
  19.7 26.1 %copy-start.9 = (s32[2]{0:T(128)S(1)}, s32[2]{0:T(128)}, u32[]{:S(2)}) copy-start(s32[2]{0:T(128)} %param.12) | copy-start | bytes 28
  19.7 26.2 %copy-start.8 = (f32[2,640]{1,0:T(2,128)S(1)}, f32[2,640]{1,0:T(2,128)}, u32[]{:S(2)}) copy-start(f32[2,640]{1,0:T(2,128)} %param.16) | copy-start | bytes 15364
  41.5 22.0 %all-to-all-start.2 = ((bf16[8,640,128]{2,1,0:T(8,128)(2,1)}), bf16[8,640,128]{2,1,0:T(8,128)(2,1)}, u32[]{:S(2)}, u32[]{:S(2)}) async-start(bf16[8,640,128]{2,1,0:T(8,128)(2,1)} %get-tuple-element.30), calls=%async_computation.2 | async-start | bytes 2621440 | tf_op jit(solution)/shard_map/all_to_all | solution.py:414
  63.5 41.6 %all-to-all-start.1 = ((bf16[8,560,128]{2,1,0:T(8,128)(2,1)}), bf16[8,560,128]{2,1,0:T(8,128)(2,1)}, u32[]{:S(2)}, u32[]{:S(2)}) async-start(bf16[8,560,128]{2,1,0:T(8,128)(2,1)} %get-tuple-element.29), calls=%async_computation.1 | async-start | bytes 2293760 | tf_op jit(solution)/shard_map/all_to_all | solution.py:414
  68.0 1.7 copy-start.6
  68.0 1.7 copy-start.7
  70.6 19.1 %copy-start.1 = (f32[640,7]{1,0:T(8,128)S(1)}, f32[640,7]{1,0:T(8,128)}, u32[]{:S(2)}) copy-start(f32[640,7]{1,0:T(8,128)} %copy.38) | copy-start | bytes 53764
  105.1 14.4 %copy-start.10 = (s32[2]{0:T(128)S(1)}, s32[2]{0:T(128)}, u32[]{:S(2)}) copy-start(s32[2]{0:T(128)} %param.13) | copy-start | bytes 28
  118.5 6.4 %collective-permute-start.2 = (bf16[640,128]{1,0:T(8,128)(2,1)}, bf16[640,128]{1,0:T(8,128)(2,1)S(1)}, u32[]{:S(2)}, u32[]{:S(2)}) collective-permute-start(bf16[640,128]{1,0:T(8,128)(2,1)} %get-tuple-element.38), channel_id=1, source_target_pairs={{0,8},{8,16},{16,24},{24,32},{32,40},{40,48},{48,56},{56,64},{64,7... | collective-permute-start | bytes 491528 | tf_op jit(solution)/shard_map/ppermute | solution.py:454
  119.3 5.6 %collective-permute-start.3 = (bf16[640,128]{1,0:T(8,128)(2,1)}, bf16[640,128]{1,0:T(8,128)(2,1)S(1)}, u32[]{:S(2)}, u32[]{:S(2)}) collective-permute-start(bf16[640,128]{1,0:T(8,128)(2,1)} %get-tuple-element.39), channel_id=1, source_target_pairs={{0,120},{8,0},{16,8},{24,16},{32,24},{40,32},{48,40},{56,48},{64,5... | collective-permute-start | bytes 491528 | tf_op jit(solution)/shard_map/ppermute | solution.py:455
  119.6 34.2 %collective-permute-start.6 = (bf16[640,128]{1,0:T(8,128)(2,1)}, bf16[640,128]{1,0:T(8,128)(2,1)}, u32[]{:S(2)}, u32[]{:S(2)}) collective-permute-start(bf16[640,128]{1,0:T(8,128)(2,1)} %get-tuple-element.40), channel_id=1, source_target_pairs={{0,1},{1,2},{2,3},{3,4},{4,5},{5,6},{6,7},{8,9},{9,10},{10,11},{11... | collective-permute-start | bytes 491528 | tf_op jit(solution)/shard_map/ppermute | solution.py:456
  123.6 30.2 %collective-permute-start.7 = (bf16[640,128]{1,0:T(8,128)(2,1)}, bf16[640,128]{1,0:T(8,128)(2,1)}, u32[]{:S(2)}, u32[]{:S(2)}) collective-permute-start(bf16[640,128]{1,0:T(8,128)(2,1)} %get-tuple-element.41), channel_id=1, source_target_pairs={{1,0},{2,1},{3,2},{4,3},{5,4},{6,5},{7,6},{9,8},{10,9},{11,10},{12... | collective-permute-start | bytes 491528 | tf_op jit(solution)/shard_map/ppermute | solution.py:457
  124.9 28.8 %copy-start.2 = (bf16[640,128]{1,0:T(8,128)(2,1)}, bf16[640,128]{1,0:T(8,128)(2,1)S(1)}, u32[]{:S(2)}) copy-start(bf16[640,128]{1,0:T(8,128)(2,1)S(1)} %add.49.near_ref) | copy-start | bytes 491524
  125.0 28.8 %collective-permute-start.5 = (bf16[640,128]{1,0:T(8,128)(2,1)S(1)}, bf16[640,128]{1,0:T(8,128)(2,1)}, u32[]{:S(2)}, u32[]{:S(2)}) collective-permute-start(bf16[640,128]{1,0:T(8,128)(2,1)S(1)} %add.49.near_ref), channel_id=1, source_target_pairs={{1,0},{2,1},{3,2},{4,3},{5,4},{6,5},{7,6},{9,8},{10,9},{11,10},{12... | collective-permute-start | bytes 491528 | tf_op jit(solution)/shard_map/ppermute | solution.py:460
  126.3 27.5 %collective-permute-start.4 = (bf16[640,128]{1,0:T(8,128)(2,1)S(1)}, bf16[640,128]{1,0:T(8,128)(2,1)}, u32[]{:S(2)}, u32[]{:S(2)}) collective-permute-start(bf16[640,128]{1,0:T(8,128)(2,1)S(1)} %add.49.near_ref), channel_id=1, source_target_pairs={{0,1},{1,2},{2,3},{3,4},{4,5},{5,6},{6,7},{8,9},{9,10},{10,11},{11... | collective-permute-start | bytes 491528 | tf_op jit(solution)/shard_map/ppermute | solution.py:459
  131.6 22.1 %all-to-all-start.3 = ((f32[128,1,128]{2,1,0:T(1,128)}), f32[128,1,128]{2,1,0:T(1,128)S(1)}, u32[]{:S(2)}, u32[]{:S(2)}) async-start(f32[128,1,128]{2,1,0:T(1,128)} %bitcast.42), calls=%async_computation.3 | async-start | bytes 131072 | tf_op jit(solution)/shard_map/all_to_all | solution.py:404
  153.7 0.6 copy-start.3
